TPU v7x, 32 devices: a whole 2x2x4 slice. The times are simulated.
32 devices in a mesh: wide: 8 (over z, x), narrow: 4 (over y, core).
Axes of the slice: x: 2, y: 2, z: 4, core: 2. Of those that a mesh axis runs over, the one named last changes fastest.
Arguments:
- tokens: bfloat16 [2, 32, 256, 640], P(None, ('wide', 'narrow')), may hold values from -6 to 6
- cotangent: bfloat16 [2, 32, 256, 640], P(None, ('wide', 'narrow')), may hold values from -6 to 6
- lengths: int32 [2, 32], P(None, ('wide', 'narrow')), may hold values from 32 to 1056, as said below
- offsets: int32 [2, 32], P(None, ('wide', 'narrow')), may hold values from 0 to 928, as said below
- attn_weight: float32 [640, 2560], P(None, ('wide', 'narrow'))
- attn_first: float32 [640, 2560], P(None, ('wide', 'narrow'))
- attn_second: float32 [640, 2560], P(None, ('wide', 'narrow'))
- up_weight: float32 [640, 2560], P(None, ('wide', 'narrow')), may hold values from -0.25 to 0.25
- up_first: float32 [640, 2560], P(None, ('wide', 'narrow')), may hold values from -24 to 24
- up_second: float32 [640, 2560], P(None, ('wide', 'narrow')), may hold values from 1.47456 to 5.89824
- down_weight: float32 [640, 2560], P(None, ('wide', 'narrow')), may hold values from -0.125 to 0.125
- down_first: float32 [640, 2560], P(None, ('wide', 'narrow')), may hold values from -48 to 48
- down_second: float32 [640, 2560], P(None, ('wide', 'narrow')), may hold values from 5.89824 to 23.59296
- vectors: float32 [13, 640], replicated
- vec_first: float32 [13, 640], replicated, may hold values from -48 to 48
- vec_second: float32 [13, 640], replicated, may hold values from 5.89824 to 23.59296
Outputs:
- output: bfloat16 [2, 32, 256, 640], P(None, ('wide', 'narrow'))
- input_grad: bfloat16 [2, 32, 256, 640], P(None, ('wide', 'narrow'))
- attn_grad: float32 [640, 2560], P(None, ('wide', 'narrow'))
- up_grad: float32 [640, 2560], P(None, ('wide', 'narrow'))
- down_grad: float32 [640, 2560], P(None, ('wide', 'narrow'))
- vector_grad: float32 [13, 640], replicated
- attn_second_new: float32 [640, 2560], P(None, ('wide', 'narrow'))
- up_second_new: float32 [640, 2560], P(None, ('wide', 'narrow'))
- down_second_new: float32 [640, 2560], P(None, ('wide', 'narrow'))
- vec_second_new: float32 [13, 640], replicated
- attn_new: float32 [640, 2560], P(None, ('wide', 'narrow'))
- up_new: float32 [640, 2560], P(None, ('wide', 'narrow'))
- down_new: float32 [640, 2560], P(None, ('wide', 'narrow'))
- vectors_new: float32 [13, 640], replicated
Inputs may be any that keep to these rules, and one draw needn't show every extreme that they name: `lengths`: lengths are heavy-tailed; some window holds a protein of each extreme length. `offsets`: A window of a protein no longer than 256 starts at 0; a longer protein's window starts at least 128 positions before its end. So 256 // 8 to 256 keys of a window are visible, and some window has exactly 32.
All inputs are finite; a program needn't handle non-finite values.
Results may differ from a plain program's by a relative error of at most 0.014.
Values may be sent and summed in bfloat16 or wider, within the bound.
No kernel may reach another device: no remote copies, remote signals or barrier semaphores. Data moves between devices by JAX's collectives and lax.ppermute only.
A program may use at most 128 MiB of HBM per device.

v0:
```python
import jax
import jax.numpy as jnp
from jax import lax
from jax.sharding import PartitionSpec as P

D = 640
HEADS = 20
HEAD_DIM = 32
FF = 2560
SEQ = 256
STEP = 10


def layer_norm(inputs, gain_row, shift_row):
    centered = inputs - jnp.mean(inputs, axis=-1, keepdims=True)
    scaled = centered * lax.rsqrt(jnp.mean(centered * centered, axis=-1, keepdims=True) + 1e-05)
    return scaled * gain_row + shift_row


def rotary(inputs):
    position = jnp.arange(SEQ, dtype=jnp.float32)
    frequency = 10000.0 ** (-jnp.arange(0, HEAD_DIM, 2, dtype=jnp.float32) / HEAD_DIM)
    angles = position[:, None] * frequency[None, :]
    angles = jnp.concatenate([angles, angles], axis=-1)[:, None, :]
    half_dim = HEAD_DIM // 2
    turned = jnp.concatenate([-inputs[..., half_dim:], inputs[..., :half_dim]], axis=-1)
    return inputs * jnp.cos(angles) + turned * jnp.sin(angles)


def gelu_exact(pre_values):
    return jax.nn.gelu(pre_values, approximate=False)


def contract_rows(left, right):
    return lax.dot_general(
        left, right, (((0,), (0,)), ((), ())), preferred_element_type=jnp.float32
    )


def contract_cols(left, right):
    return lax.dot_general(
        left, right, (((1,), (1,)), ((), ())), preferred_element_type=jnp.float32
    )


def masked_scores(queries, keys_rot, key_count):
    raw_scores = jnp.einsum(
        "qhe,khe->hqk", queries, keys_rot, preferred_element_type=jnp.float32
    ) * HEAD_DIM ** (-0.5)
    visible = jnp.arange(SEQ, dtype=jnp.int32) < key_count
    return jnp.where(visible[None, None, :], raw_scores, -1000000000.0)


def attend_forward(queries, keys_rot, values, key_count):
    scores = masked_scores(queries, keys_rot, key_count)
    row_max = jnp.max(scores, axis=-1, keepdims=True)
    exponent = jnp.exp(scores - row_max)
    row_total = jnp.sum(exponent, axis=-1, keepdims=True)
    probabilities = (exponent / row_total).astype(jnp.bfloat16)
    mixed_heads = jnp.einsum(
        "hqk,khe->qhe", probabilities, values, preferred_element_type=jnp.float32
    )
    logsum = (row_max + jnp.log(row_total))[..., 0]
    return (mixed_heads, logsum)


def attend_backward(queries, keys_rot, values, key_count, logsum, grad_mixed):
    scores = masked_scores(queries, keys_rot, key_count)
    probabilities = jnp.exp(scores - logsum[..., None])
    prob_low = probabilities.astype(jnp.bfloat16)
    grad_probs = jnp.einsum("qhe,khe->hqk", grad_mixed, values, preferred_element_type=jnp.float32)
    inner_sum = jnp.sum(probabilities * grad_probs, axis=-1, keepdims=True)
    grad_scores = (probabilities * (grad_probs - inner_sum)).astype(jnp.bfloat16)
    grad_queries = jnp.einsum(
        "hqk,khe->qhe", grad_scores, keys_rot, preferred_element_type=jnp.float32
    ) * HEAD_DIM ** (-0.5)
    grad_keys = jnp.einsum(
        "hqk,qhe->khe", grad_scores, queries, preferred_element_type=jnp.float32
    ) * HEAD_DIM ** (-0.5)
    grad_values = jnp.einsum(
        "hqk,qhe->khe", prob_low, grad_mixed, preferred_element_type=jnp.float32
    )
    return (grad_queries, grad_keys, grad_values)


def forward_pass(matrices, vectors, inputs, counts):
    attn_mat, up_mat, down_mat = matrices
    windows = inputs.shape[0]
    row_count = windows * SEQ
    flat_rows = inputs.reshape(row_count, D).astype(jnp.float32)
    hidden = layer_norm(flat_rows, vectors[0], vectors[1]).astype(jnp.bfloat16)
    project = jnp.dot(hidden, attn_mat[:, : 3 * D], preferred_element_type=jnp.float32) + vectors[
        2:5
    ].reshape(3 * D)
    split_q = project[:, :D].reshape(windows, SEQ, HEADS, HEAD_DIM)
    split_k = project[:, D : 2 * D].reshape(windows, SEQ, HEADS, HEAD_DIM)
    queries = rotary(split_q).astype(jnp.bfloat16)
    keys_rot = rotary(split_k).astype(jnp.bfloat16)
    values = project[:, 2 * D :].astype(jnp.bfloat16).reshape(windows, SEQ, HEADS, HEAD_DIM)
    mixed_heads, logsum = jax.vmap(attend_forward)(queries, keys_rot, values, counts)
    mixed_low = mixed_heads.reshape(row_count, D).astype(jnp.bfloat16)
    middle = (
        flat_rows
        + jnp.dot(mixed_low, attn_mat[:, 3 * D :], preferred_element_type=jnp.float32)
        + vectors[5]
    )
    normed = layer_norm(middle, vectors[6], vectors[7]).astype(jnp.bfloat16)
    pre_act = jnp.dot(normed, up_mat, preferred_element_type=jnp.float32) + vectors[9:].reshape(FF)
    active = gelu_exact(pre_act).astype(jnp.bfloat16)
    result = middle + contract_cols(active, down_mat) + vectors[8]
    saved_state = (
        flat_rows,
        hidden,
        split_q,
        split_k,
        queries,
        keys_rot,
        values,
        logsum,
        mixed_low,
        middle,
        normed,
        pre_act,
        active,
    )
    return (result.reshape(windows, SEQ, D).astype(jnp.bfloat16), saved_state)


def backward_pass(matrices, vectors, saved_state, counts, back_rows):
    attn_mat, up_mat, down_mat = matrices
    (
        flat_rows,
        hidden,
        split_q,
        split_k,
        queries,
        keys_rot,
        values,
        logsum,
        mixed_low,
        middle,
        normed,
        pre_act,
        active,
    ) = saved_state
    windows = back_rows.shape[0]
    row_count = windows * SEQ
    back_flat = back_rows.reshape(row_count, D)
    back_wide = back_flat.astype(jnp.float32)
    grad_down = contract_rows(back_flat, active)
    grad_active = jnp.dot(back_flat, down_mat, preferred_element_type=jnp.float32)
    unused, gelu_pull = jax.vjp(gelu_exact, pre_act)
    grad_pre = gelu_pull(grad_active)[0].astype(jnp.bfloat16)
    grad_up = contract_rows(normed, grad_pre)
    grad_bias_up = jnp.sum(grad_pre.astype(jnp.float32), axis=0)
    grad_normed = contract_cols(grad_pre, up_mat)
    unused, second_pull = jax.vjp(layer_norm, middle, vectors[6], vectors[7])
    grad_mid_part, grad_gain_two, grad_shift_two = second_pull(grad_normed)
    grad_middle = back_wide + grad_mid_part
    grad_branch = grad_middle.astype(jnp.bfloat16)
    grad_out_proj = contract_rows(mixed_low, grad_branch)
    grad_mixed = (
        contract_cols(grad_branch, attn_mat[:, 3 * D :])
        .astype(jnp.bfloat16)
        .reshape(windows, SEQ, HEADS, HEAD_DIM)
    )
    grad_q_rot, grad_k_rot, grad_values = jax.vmap(attend_backward)(
        queries, keys_rot, values, counts, logsum, grad_mixed
    )
    unused, rope_query = jax.vjp(rotary, split_q)
    unused, rope_key = jax.vjp(rotary, split_k)
    grad_q_pre = rope_query(grad_q_rot)[0].reshape(row_count, D)
    grad_k_pre = rope_key(grad_k_rot)[0].reshape(row_count, D)
    grad_project = jnp.concatenate(
        [grad_q_pre, grad_k_pre, grad_values.reshape(row_count, D)], axis=1
    ).astype(jnp.bfloat16)
    grad_in_proj = contract_rows(hidden, grad_project)
    grad_bias_proj = jnp.sum(grad_project.astype(jnp.float32), axis=0).reshape(3, D)
    grad_hidden = contract_cols(grad_project, attn_mat[:, : 3 * D])
    unused, first_pull = jax.vjp(layer_norm, flat_rows, vectors[0], vectors[1])
    grad_flat, grad_gain_one, grad_shift_one = first_pull(grad_hidden)
    input_grad = (grad_middle + grad_flat).reshape(windows, SEQ, D).astype(jnp.bfloat16)
    grad_attn = jnp.concatenate([grad_in_proj, grad_out_proj], axis=1)
    head_rows = jnp.stack([grad_gain_one, grad_shift_one])
    tail_rows = jnp.stack(
        [jnp.sum(grad_middle, axis=0), grad_gain_two, grad_shift_two, jnp.sum(back_wide, axis=0)]
    )
    vec_grad = jnp.concatenate(
        [head_rows, grad_bias_proj, tail_rows, grad_bias_up.reshape(4, D)], axis=0
    )
    return (input_grad, (grad_attn, grad_up, grad_down), vec_grad)


def adamw(weight, first_moment, second_moment, gradient, rate_value):
    first_new = 0.9 * first_moment + 0.1 * gradient
    second_new = 0.999 * second_moment + 0.001 * gradient * gradient
    corrected = first_new / (1.0 - 0.9**STEP) / (jnp.sqrt(second_new / (1.0 - 0.999**STEP)) + 1e-08)
    return (second_new, weight - rate_value * (corrected + 0.01 * weight))


def per_device(
    tokens,
    cotangent,
    lengths,
    offsets,
    attn_weight,
    attn_first,
    attn_second,
    up_weight,
    up_first,
    up_second,
    down_weight,
    down_first,
    down_second,
    vectors,
    vec_first,
    vec_second,
):
    shards = (
        attn_weight.astype(jnp.bfloat16),
        up_weight.astype(jnp.bfloat16),
        down_weight.astype(jnp.bfloat16),
    )
    counts = jnp.minimum(lengths - offsets, SEQ)
    grad_mats = (
        jnp.zeros((D, 4 * D), jnp.float32),
        jnp.zeros((D, FF), jnp.float32),
        jnp.zeros((D, FF), jnp.float32),
    )
    grad_vec = jnp.zeros((13, D), jnp.float32)
    output_list = []
    input_list = []
    for micro_index in range(tokens.shape[0]):
        forward_mats = (
            lax.all_gather(shards[0], ("wide", "narrow"), axis=1, tiled=True),
            lax.all_gather(shards[1], ("wide", "narrow"), axis=1, tiled=True),
            lax.all_gather(shards[2], ("wide", "narrow"), axis=1, tiled=True),
        )
        result, saved_state = forward_pass(
            forward_mats, vectors, tokens[micro_index], counts[micro_index]
        )
        backward_mats = (
            lax.all_gather(shards[0], ("wide", "narrow"), axis=1, tiled=True),
            lax.all_gather(shards[1], ("wide", "narrow"), axis=1, tiled=True),
            lax.all_gather(shards[2], ("wide", "narrow"), axis=1, tiled=True),
        )
        input_grad, mat_grads, vec_grad = backward_pass(
            backward_mats, vectors, saved_state, counts[micro_index], cotangent[micro_index]
        )
        grad_mats = tuple((grad_mats[member] + mat_grads[member] for member in range(3)))
        grad_vec = grad_vec + vec_grad
        output_list.append(result)
        input_list.append(input_grad)
    grad_mats = lax.psum_scatter(grad_mats, ("wide", "narrow"), scatter_dimension=1, tiled=True)
    grad_vec = lax.psum(grad_vec, ("wide", "narrow"))
    attn_second_new, attn_new = adamw(attn_weight, attn_first, attn_second, grad_mats[0], 0.1)
    up_second_new, up_new = adamw(up_weight, up_first, up_second, grad_mats[1], 0.1)
    down_second_new, down_new = adamw(down_weight, down_first, down_second, grad_mats[2], 0.1)
    vec_second_new, vectors_new = adamw(vectors, vec_first, vec_second, grad_vec, 0.5)
    return (
        jnp.stack(output_list),
        jnp.stack(input_list),
        grad_mats[0],
        grad_mats[1],
        grad_mats[2],
        grad_vec,
        attn_second_new,
        up_second_new,
        down_second_new,
        vec_second_new,
        attn_new,
        up_new,
        down_new,
        vectors_new,
    )


def solution(mesh):
    in_specs = (
        P(None, ("wide", "narrow"), None, None),
        P(None, ("wide", "narrow"), None, None),
        P(None, ("wide", "narrow")),
        P(None, ("wide", "narrow")),
        P(None, ("wide", "narrow")),
        P(None, ("wide", "narrow")),
        P(None, ("wide", "narrow")),
        P(None, ("wide", "narrow")),
        P(None, ("wide", "narrow")),
        P(None, ("wide", "narrow")),
        P(None, ("wide", "narrow")),
        P(None, ("wide", "narrow")),
        P(None, ("wide", "narrow")),
        P(),
        P(),
        P(),
    )
    out_specs = (
        P(None, ("wide", "narrow"), None, None),
        P(None, ("wide", "narrow"), None, None),
        P(None, ("wide", "narrow")),
        P(None, ("wide", "narrow")),
        P(None, ("wide", "narrow")),
        P(),
        P(None, ("wide", "narrow")),
        P(None, ("wide", "narrow")),
        P(None, ("wide", "narrow")),
        P(),
        P(None, ("wide", "narrow")),
        P(None, ("wide", "narrow")),
        P(None, ("wide", "narrow")),
        P(),
    )
    return jax.shard_map(
        per_device, mesh=mesh, in_specs=in_specs, out_specs=out_specs, check_vma=False
    )
```

profile of v0, /device:TPU:0, one launch (start us, length us, event | category | flops | bytes accessed | tf_op | source)
XLA Modules:
  0.0 679.7 jit_solution(18184182134111048022)
XLA Ops:
  7.2 1.6 convert_element_type.174
  8.9 1.6 convert_element_type.183
  12.0 1.5 slice_reduce_fusion
  16.1 1.2 convert_reduce_fusion.7
  17.4 1.4 fusion.66
  19.0 54.5 %all-gather.4.cloned.1.call-done = bf16[640,2560]{0,1:T(8,128)(2,1)} async-done(((bf16[640,80]{0,1:T(8,128)(2,1)}), bf16[640,2560]{0,1:T(8,128)(2,1)}) %all-gather.4.cloned.1.call-update) | async-done | bytes 3276816 | tf_op jit(solution)/shard_map/all_gather | solution.py:235
  73.5 3.0 convolution_add_fusion.3
  76.5 2.4 convolution_add_fusion.4
  80.4 1.9 slice.265
  82.2 2.2 fusion.138
  84.7 1.9 copy.177
  86.6 1.3 copy.178
  88.8 1.3 fusion.147
  91.0 1.5 copy-done
  92.5 1.0 fusion.35
  93.5 0.9 copy-done.57
  95.3 1.4 fusion.145
  97.5 1.5 copy-done.1
  99.0 1.0 fusion.34
  100.9 34.2 %all-gather.6.cloned.1.call-done = bf16[640,2560]{0,1:T(8,128)(2,1)} async-done(((bf16[640,80]{0,1:T(8,128)(2,1)}), bf16[640,2560]{0,1:T(8,128)(2,1)}) %all-gather.6.cloned.1.call-update) | async-done | bytes 3276816 | tf_op jit(solution)/shard_map/all_gather | solution.py:236
  135.1 9.9 %multiply_convert_fusion.3 = (bf16[256,2560]{1,0:T(8,128)(2,1)S(1)}, f32[256,2560]{1,0:T(8,128)}, f32[256,2560]{1,0:T(8,128)}) fusion(f32[2560]{0:T(1024)S(1)} %add.315, bf16[640,2560]{0,1:T(8,128)(2,1)} %all-gather.6.cloned.1.call-done, f32[256,640]{1,0:T(8,128)S(1)} %get-tuple-element.170, f32[640]{0:T(1024)S(1)} %get-tuple-element.95, ...), kind=kOutput, calls=%fused_computation.48 | convolution fusion | flops 882933760 | bytes 10503168 | tf_op jit(solution)/shard_map/dot_general | solution.py:108
  145.0 1.2 fusion.93
  146.2 1.2 copy-done.61
  147.4 9.8 %multiply_convert_fusion.2 = (bf16[256,2560]{1,0:T(8,128)(2,1)S(1)}, f32[256,2560]{1,0:T(8,128)}, f32[256,2560]{1,0:T(8,128)}) fusion(f32[2560]{0:T(1024)S(1)} %add.315, bf16[640,2560]{0,1:T(8,128)(2,1)S(1)} %copy-done.61, f32[256,640]{1,0:T(8,128)S(1)} %get-tuple-element.165, f32[256]{0:T(256)S(1)} %fusion.118, f32[256]{0:T(256)S(1)} %broadcast_multiply_fusion.6, ...), kind=kOutput, calls=%fused_computation.35 | convolution fusion | flops 882933760 | bytes 10503168 | tf_op jit(solution)/shard_map/dot_general | solution.py:108
  157.2 1.0 copy-done.36
  158.2 4.0 convolution_add_fusion
  162.3 144.0 %reduce-scatter.14.cloned.1.call-done = f32[80,640]{1,0:T(8,128)} async-done(((f32[2560,640]{1,0:T(8,128)}), f32[80,640]{1,0:T(8,128)}) %reduce-scatter.14.cloned.1.call-update) | async-done | bytes 204816
  306.3 1.9 multiply_subtract_fusion
  308.2 57.0 %all-gather.8.cloned.1.call-done = bf16[640,2560]{0,1:T(8,128)(2,1)} async-done(((bf16[640,80]{0,1:T(8,128)(2,1)}), bf16[640,2560]{0,1:T(8,128)(2,1)}) %all-gather.8.cloned.1.call-update) | async-done | bytes 3276816 | tf_op jit(solution)/shard_map/all_gather | solution.py:237
  365.2 5.2 convert_reduce_fusion.1
  370.5 1.3 fusion.127
  371.8 1.0 copy-done.59
  374.4 1.8 convert_reduce_fusion
  376.3 1.1 copy-done.31
  377.3 4.1 add_bitcast_fusion
  381.8 3.7 fusion.149
  385.4 1.5 multiply_reduce_fusion.2
  387.0 1.6 fusion.134
  388.6 2.4 convolution_convert_fusion.1
  391.0 1.9 copy.189
  392.9 2.4 convolution_convert_fusion
  395.2 1.9 copy.193
  397.1 4.1 multiply_reduce_fusion.1
  401.3 1.5 multiply_convert_fusion.1
  404.9 1.2 multiply_reduce_fusion
  406.1 1.4 multiply_convert_fusion
  413.1 1.1 fusion.119
  414.2 0.9 fusion.38
  415.2 1.1 fusion.120
  416.2 3.2 maximum_add_fusion
  419.5 8.2 %copy.223 = f32[640,2560]{0,1:T(8,128)} copy(f32[640,2560]{1,0:T(8,128)} %maximum_add_fusion) | data formatting | bytes 13107200
  427.8 1.5 convert_reduce_fusion.3
  429.3 1.5 convert_reduce_fusion.2
  430.9 3.2 fusion.24
  434.2 1.2 fusion.67
  435.5 1.0 convert_reduce_fusion.4
  436.7 40.3 %psum.7 = f32[13,640]{1,0:T(8,128)S(1)} all-reduce(f32[13,640]{1,0:T(8,128)S(1)} %add.344), channel_id=1, replica_groups=mesh['wide'=8,'narrow'=4] {'wide','narrow'}, use_global_device_ids=true, to_apply=%region_41.42 | all-reduce | flops 8320 | bytes 66560 | tf_op jit(solution)/shard_map/psum | solution.py:255
  477.1 3.7 fusion.44
  481.0 1.2 fusion.45
  482.2 0.9 pad_maximum_fusion.2
  485.4 40.5 %reduce-scatter.12.cloned.1.call-done = f32[80,640]{1,0:T(8,128)} async-done(((f32[2560,640]{1,0:T(8,128)}), f32[80,640]{1,0:T(8,128)}) %reduce-scatter.12.cloned.1.call-update) | async-done | bytes 204816
  525.9 2.0 multiply_subtract_fusion.1
  527.9 142.8 %reduce-scatter.10.cloned.1.call-done = f32[80,640]{1,0:T(8,128)} async-done(((f32[2560,640]{1,0:T(8,128)}), f32[80,640]{1,0:T(8,128)}) %reduce-scatter.10.cloned.1.call-update) | async-done | bytes 204816
  670.7 1.8 multiply_subtract_fusion.2
  (225 shorter events, 22.7 us)
Async XLA Ops:
  7.2 66.3 %all-gather.4.cloned.1.call-start = ((), (), s32[]{:S(2)}) async-start(), calls=%async_computation.3 | async-start | bytes 3379200 | tf_op jit(solution)/shard_map/all_gather | solution.py:235
  8.8 126.2 %all-gather.6.cloned.1.call-start = ((), (), s32[]{:S(2)}) async-start(), calls=%async_computation.4 | async-start | bytes 3379200 | tf_op jit(solution)/shard_map/all_gather | solution.py:236
  10.5 295.8 %reduce-scatter.14.cloned.1.call-start = ((), (), s32[]{:S(2)}) async-start(), calls=%async_computation.8 | async-start | bytes 6758400
  73.5 3.0 copy-start.2
  73.5 3.0 copy-start.56
  88.8 1.4 copy-start.10
  88.8 1.4 copy-start.12
  88.8 6.5 copy-start.6
  88.8 6.4 copy-start.8
  90.2 2.3 copy-start
  90.2 2.3 copy-start.35
  92.5 1.9 copy-start.57
  93.5 3.1 copy-start.40
  95.0 290.4 %copy-start.4 = (f32[256,640]{1,0:T(8,128)}, f32[256,640]{1,0:T(8,128)S(1)}, u32[]{:S(2)}) copy-start(f32[256,640]{1,0:T(8,128)S(1)} %get-tuple-element.170) | copy-start | bytes 1966084
  96.7 2.4 copy-start.1
  96.7 2.4 copy-start.33
  100.0 35.0 %copy-start.42 = (bf16[20,32,256]{2,1,0:T(8,128)(2,1)}, bf16[20,32,256]{2,1,0:T(8,128)(2,1)S(1)}, u32[]{:S(2)}) copy-start(bf16[20,32,256]{2,1,0:T(8,128)(2,1)S(1)} %fusion.34) | copy-start | bytes 983044
  135.1 9.9 %copy-start.3 = (bf16[2,1,256,640]{3,2,1,0:T(8,128)(2,1)S(1)}, bf16[2,1,256,640]{3,2,1,0:T(8,128)(2,1)}, u32[]{:S(2)}) copy-start(bf16[2,1,256,640]{3,2,1,0:T(8,128)(2,1)} %param.17) | copy-start | bytes 1966084
  145.0 1.2 copy-start.29
  145.0 2.4 copy-start.61
  162.2 144.1 %copy-start.46 = (f32[640,80]{0,1:T(8,128)S(1)}, f32[640,80]{0,1:T(8,128)}, u32[]{:S(2)}) copy-start(f32[640,80]{0,1:T(8,128)} %param.26) | copy-start | bytes 614404
  162.2 144.1 %copy-start.47 = (f32[640,80]{0,1:T(8,128)S(1)}, f32[640,80]{0,1:T(8,128)}, u32[]{:S(2)}) copy-start(f32[640,80]{0,1:T(8,128)} %param.27) | copy-start | bytes 614404
  162.2 144.1 %copy-start.48 = (f32[640,80]{0,1:T(8,128)S(1)}, f32[640,80]{0,1:T(8,128)}, u32[]{:S(2)}) copy-start(f32[640,80]{0,1:T(8,128)} %param.28) | copy-start | bytes 614404
  162.2 203.0 %all-gather.8.cloned.1.call-start = ((), (), s32[]{:S(2)}) async-start(), calls=%async_computation.5 | async-start | bytes 3379200 | tf_op jit(solution)/shard_map/all_gather | solution.py:237
  308.2 217.7 %reduce-scatter.12.cloned.1.call-start = ((), (), s32[]{:S(2)}) async-start(), calls=%async_computation.7 | async-start | bytes 6758400
  370.4 1.4 copy-start.37
  370.5 2.4 copy-start.59
  370.5 3.2 copy-start.63
  370.5 3.9 copy-start.64
  381.5 289.2 %reduce-scatter.10.cloned.1.call-start = ((), (), s32[]{:S(2)}) async-start(), calls=%async_computation.6 | async-start | bytes 6758400
  381.7 3.7 copy-start.32
  381.7 3.7 copy-start.62
  397.1 4.1 slice-start
  397.1 4.2 slice-start.1
  397.1 7.2 %slice-start.2 = ((s8[5242880]{0:T(1024)(128)(4,1)}), s8[4194304]{0:T(1024)(128)(4,1)S(1)}, s32[]{:S(2)}) async-start(s8[5242880]{0:T(1024)(128)(4,1)} %bitcast.246), calls=%async_computation.11 | async-start | bytes 8388608
  401.3 1.5 copy-start.13
  401.3 3.0 slice-start.3
  406.1 1.4 copy-start.9
  409.3 1.4 copy-start.43
  412.2 3.0 copy-start.16
  412.2 3.0 copy-start.18
  413.1 1.1 copy-start.24
  413.1 1.1 copy-start.14
  415.1 1.1 copy-start.22
  430.9 3.2 copy-start.17
  430.9 3.2 copy-start.19
  430.9 3.2 copy-start.23
  430.9 3.3 copy-start.58
  434.2 1.3 copy-start.25
  435.4 41.6 %copy-start.55 = (f32[640]{0:T(1024)S(1)}, f32[640]{0:T(1024)}, u32[]{:S(2)}) copy-start(f32[640]{0:T(1024)} %get-tuple-element.94) | copy-start | bytes 7684
  477.0 7.7 %copy-start.49 = (f32[13,640]{1,0:T(8,128)}, f32[13,640]{1,0:T(8,128)S(1)}, u32[]{:S(2)}) copy-start(f32[13,640]{1,0:T(8,128)S(1)} %psum.7) | copy-start | bytes 99844
  477.1 3.7 copy-start.5
  477.1 3.7 copy-start.30
  477.1 3.9 copy-start.60
  481.0 2.1 copy-start.26
  481.0 2.1 copy-start.28
  481.0 2.1 copy-start.54
  483.1 1.6 copy-start.50
  483.1 1.6 copy-start.51
  483.1 1.6 copy-start.52
  483.1 42.7 %copy-start.38 = (f32[640,80]{0,1:T(8,128)S(1)}, f32[640,80]{0,1:T(8,128)}, u32[]{:S(2)}) copy-start(f32[640,80]{0,1:T(8,128)} %param.23) | copy-start | bytes 614404
  483.8 186.9 %copy-start.39 = (f32[640,80]{0,1:T(8,128)S(1)}, f32[640,80]{0,1:T(8,128)}, u32[]{:S(2)}) copy-start(f32[640,80]{0,1:T(8,128)} %param.20) | copy-start | bytes 614404
  483.8 186.9 %copy-start.44 = (f32[640,80]{0,1:T(8,128)S(1)}, f32[640,80]{0,1:T(8,128)}, u32[]{:S(2)}) copy-start(f32[640,80]{0,1:T(8,128)} %param.21) | copy-start | bytes 614404
  483.8 186.9 %copy-start.45 = (f32[640,80]{0,1:T(8,128)S(1)}, f32[640,80]{0,1:T(8,128)}, u32[]{:S(2)}) copy-start(f32[640,80]{0,1:T(8,128)} %param.22) | copy-start | bytes 614404
  (11 other events, 11.1 us)
Sparse Core Ops, SparseCore 0:
  11.4 61.9 all-gather.3
  76.9 58.1 all-gather.5
  162.3 143.8 reduce-scatter.13
  309.5 55.6 all-gather.7
  381.6 144.2 reduce-scatter.11
  528.6 142.0 reduce-scatter.9
where the time goes:
time: 690 us; the launch traced here: 680 us
  waiting for transfers between devices  473 us (69%)
  matrix products  81.1 us (12%)
  blocking collectives  40.3 us (6%)
  local copies, waits for them, and re-layouts  36.7 us (5%)
  other arithmetic  32.6 us (5%)
  between operations  15.7 us (2%)
    unnamed x9, waiting for transfers between devices  327 us
    all_gather x1, waiting for transfers between devices, per_device(): lax.all_gather(shards[2], ('wide', 'narrow'), axis=1, tiled=True)  57 us
    all_gather x1, waiting for transfers between devices, per_device(): lax.all_gather(shards[0], ('wide', 'narrow'), axis=1, tiled=True)  54.5 us
    psum x1, blocking collectives, per_device(): grad_vec = lax.psum(grad_vec, ('wide', 'narrow'))  40.3 us
    all_gather x1, waiting for transfers between devices, per_device(): lax.all_gather(shards[1], ('wide', 'narrow'), axis=1, tiled=True)  34.2 us
    unnamed x139, local copies, waits for them, and re-layouts  20.2 us
    dot_general x2, matrix products, forward_pass(): jnp.dot(normed, up_mat, preferred_element_type=jnp.float32)  19.7 us
    dot_general x8, matrix products, contract_cols(): lax.dot_general(left, right, (((1,), (1,)), ((), ())), preferred_element_...  19.2 us
  transfers between devices with their start and end apart: 6, of which 6 were waited for; matrix products, arithmetic and copies ran while one was open for 14% of the time, Pallas kernels for 0%

commit v1 on v0

v1 whole, which is shorter than its diff:
```python
import functools

import jax
import jax.numpy as jnp
from jax import lax
from jax.sharding import PartitionSpec as P

D = 640
HEADS = 20
HEAD_DIM = 32
FF = 2560
SEQ = 256
STEP = 10
AXES = ("wide", "narrow")
GROUPS = 4
GROUP_HEADS = HEADS // GROUPS
GROUP = GROUP_HEADS * HEAD_DIM
BF16 = jnp.bfloat16
F32 = jnp.float32


def nt(left, right):
    return lax.dot_general(left, right, (((1,), (1,)), ((), ())), preferred_element_type=F32)


def nn(left, right):
    return jnp.dot(left, right, preferred_element_type=F32)


def tn(left, right):
    return lax.dot_general(left, right, (((0,), (0,)), ((), ())), preferred_element_type=F32)


def pick(array, index):
    return lax.dynamic_index_in_dim(array, index, 0, keepdims=False)


def normalize(rows):
    centered = rows - jnp.mean(rows, axis=-1, keepdims=True)
    scale = lax.rsqrt(jnp.mean(centered * centered, axis=-1, keepdims=True) + 1e-05)
    return centered * scale, scale


def norm_back(grad, scaled, scale, gain):
    weighted = grad * gain
    mean_one = jnp.mean(weighted, axis=-1, keepdims=True)
    mean_two = jnp.mean(weighted * scaled, axis=-1, keepdims=True)
    return scale * (weighted - mean_one - scaled * mean_two)


def rope_tables():
    position = jnp.arange(SEQ, dtype=F32)
    frequency = 10000.0 ** (-jnp.arange(0, HEAD_DIM, 2, dtype=F32) / HEAD_DIM)
    angles = position[:, None] * frequency[None, :]
    angles = jnp.concatenate([angles, angles], axis=-1)
    return jnp.cos(angles), jnp.sin(angles)


def turn(rows, sign):
    half = HEAD_DIM // 2
    return jnp.concatenate([-sign * rows[..., half:], sign * rows[..., :half]], axis=-1)


def rotate(rows, sign):
    cos, sin = rope_tables()
    shaped = rows.reshape(-1, SEQ, GROUP_HEADS, HEAD_DIM)
    out = shaped * cos[None, :, None, :] + turn(shaped, sign) * sin[None, :, None, :]
    return out.reshape(rows.shape)


def split_heads(rows):
    return rows.reshape(-1, SEQ, GROUP_HEADS, HEAD_DIM)


def attention_forward(hidden, weight, bias, counts):
    q = rotate(nt(hidden, weight[0]) + bias[0], 1.0).astype(BF16)
    k = rotate(nt(hidden, weight[1]) + bias[1], 1.0).astype(BF16)
    v = (nt(hidden, weight[2]) + bias[2]).astype(BF16)
    scores = jnp.einsum("wqhe,wkhe->whqk", split_heads(q), split_heads(k), preferred_element_type=F32)
    scores = scores * HEAD_DIM ** (-0.5)
    visible = jnp.arange(SEQ, dtype=jnp.int32)[None, :] < counts[:, None]
    scores = jnp.where(visible[:, None, None, :], scores, -1000000000.0)
    top = jnp.max(scores, axis=-1, keepdims=True)
    exponent = jnp.exp(scores - top)
    prob = exponent / jnp.sum(exponent, axis=-1, keepdims=True)
    low = prob.astype(BF16)
    mixed = jnp.einsum("whqk,wkhe->wqhe", low, split_heads(v), preferred_element_type=F32)
    return mixed.reshape(hidden.shape[0], GROUP).astype(BF16), (q, k, v, prob)


def attention_backward(saved, grad_mixed):
    q, k, v, prob = saved
    rows = q.shape[0]
    low = prob.astype(BF16)
    do = split_heads(grad_mixed)
    dp = jnp.einsum("wqhe,wkhe->whqk", do, split_heads(v), preferred_element_type=F32)
    ds = (prob * (dp - jnp.sum(prob * dp, axis=-1, keepdims=True))).astype(BF16)
    scale = HEAD_DIM ** (-0.5)
    dq = jnp.einsum("whqk,wkhe->wqhe", ds, split_heads(k), preferred_element_type=F32) * scale
    dk = jnp.einsum("whqk,wqhe->wkhe", ds, split_heads(q), preferred_element_type=F32) * scale
    dv = jnp.einsum("whqk,wqhe->wkhe", low, do, preferred_element_type=F32)
    dq = rotate(dq.reshape(rows, GROUP), -1.0).astype(BF16)
    dk = rotate(dk.reshape(rows, GROUP), -1.0).astype(BF16)
    return dq, dk, dv.reshape(rows, GROUP).astype(BF16)


def adamw(weight, first_moment, second_moment, gradient, rate_value):
    first_new = 0.9 * first_moment + 0.1 * gradient
    second_new = 0.999 * second_moment + 0.001 * gradient * gradient
    corrected = first_new / (1.0 - 0.9**STEP) / (jnp.sqrt(second_new / (1.0 - 0.999**STEP)) + 1e-08)
    return (second_new, weight - rate_value * (corrected + 0.01 * weight))


class Layout:
    def __init__(self, total):
        self.total = total
        self.block = 4 * D // total
        self.stride = total // 4
        self.me = lax.axis_index(AXES)
        self.core = lax.rem(self.me, 2)

    def swap(self, value, mask):
        return lax.ppermute(value, AXES, [(i, i ^ mask) for i in range(self.total)])

    def shift(self, value, steps):
        pairs = [(i, (i + self.stride * steps) % self.total) for i in range(self.total)]
        return lax.ppermute(value, AXES, pairs)


class Ring(Layout):
    def __init__(self, total):
        super().__init__(total)
        self.z = self.me // 8
        self.plane = lax.rem(self.me // 2, 4)

    def along_z(self, value):
        return jnp.stack([value] + [self.shift(value, -s) for s in (1, 2, 3)])

    def in_plane(self, value):
        return [value] + [self.swap(value, 2 * r) for r in (1, 2, 3)]

    def gather_attention(self, shard):
        line = self.along_z(shard)
        groups = []
        for mine in self.in_plane(line):
            other = self.swap(mine, 1)
            first = jnp.where(self.core == 0, mine, other)
            second = jnp.where(self.core == 0, other, mine)
            chip = jnp.concatenate([first, second], axis=1)
            groups.append([pick(chip, lax.rem(part + 4 - self.z, 4)) for part in range(4)])
        return groups

    def gather_hidden(self, shard):
        line = self.along_z(shard)
        return jnp.stack(self.in_plane(line))

    def hidden_index(self):
        order = jnp.arange(16)
        place = lax.rem(self.z + lax.rem(order, 4), 4) * 4 + (self.plane ^ (order // 4))
        return place * 2 + self.core

    def scatter(self, parts):
        total = parts[0].astype(F32)
        for r in (1, 2, 3):
            total = total + self.swap(parts[r], 2 * r).astype(F32)
        low = total.astype(BF16)
        out = total[0]
        for s in (1, 2, 3):
            out = out + self.shift(low[s], s).astype(F32)
        return out

    def scatter_hidden(self, grad):
        parts = grad.reshape(4, 4, -1, D).astype(BF16)
        return self.scatter([parts[r] for r in range(4)])

    def scatter_attention(self, grads):
        parts = []
        for grad in grads:
            halves = grad.reshape(4, 2, -1, D).astype(BF16)
            mine = lax.dynamic_index_in_dim(halves, self.core, 1, keepdims=False)
            other = lax.dynamic_index_in_dim(halves, 1 - self.core, 1, keepdims=False)
            summed = (mine.astype(F32) + self.swap(other, 1).astype(F32)).astype(BF16)
            parts.append(jnp.stack([pick(summed, lax.rem(self.z + s, 4)) for s in range(4)]))
        return self.scatter(parts)


class Whole(Layout):
    def __init__(self, total):
        super().__init__(total)
        self.plane = jnp.int32(0)

    def gather(self, shard):
        return lax.all_gather(shard, AXES, axis=0, tiled=True)

    def gather_attention(self, shard):
        full = self.gather(shard).reshape(4, 4, GROUP, D)
        return [[full[part, r] for part in range(4)] for r in range(4)]

    def gather_hidden(self, shard):
        full = lax.all_gather(shard, AXES, axis=0).reshape(self.total // 2, 2, -1, D)
        return lax.dynamic_index_in_dim(full, self.core, 1, keepdims=False)

    def hidden_index(self):
        return jnp.arange(self.total // 2) * 2 + self.core

    def scatter_hidden(self, grad):
        halves = grad.reshape(self.total // 2, 1, -1, D)
        full = jnp.where(jnp.arange(2)[None, :, None, None] == self.core, halves, 0.0)
        return lax.psum_scatter(full.reshape(-1, D), AXES, scatter_dimension=0, tiled=True)

    def scatter_attention(self, grads):
        full = jnp.stack(grads, axis=1).reshape(4 * D, D)
        return lax.psum_scatter(full, AXES, scatter_dimension=0, tiled=True)


def per_device(
    total,
    tokens,
    cotangent,
    lengths,
    offsets,
    attn_weight,
    attn_first,
    attn_second,
    up_weight,
    up_first,
    up_second,
    down_weight,
    down_first,
    down_second,
    vectors,
    vec_first,
    vec_second,
):
    lay = Ring(total) if total == 32 else Whole(total)
    counts = jnp.minimum(lengths - offsets, SEQ).reshape(-1)
    rows = counts.shape[0] * SEQ

    attn_shard = attn_weight.T.astype(BF16)
    up_shard = up_weight.T.astype(BF16)
    down_shard = down_weight.T.astype(BF16)
    attn_groups = lay.gather_attention(attn_shard)
    up_full = lay.gather_hidden(up_shard).reshape(FF // 2, D)
    down_full = lay.gather_hidden(down_shard).reshape(FF // 2, D)

    flat = tokens.reshape(rows, D).astype(F32)
    back = cotangent.reshape(rows, D)
    back_both = jnp.concatenate([back, lay.swap(back, 1)])
    scaled_one, scale_one = normalize(flat)
    hidden = (scaled_one * vectors[0] + vectors[1]).astype(BF16)

    bias = vectors[2:5].reshape(3, GROUPS, GROUP)
    mixed, saved = [], []
    for r in range(GROUPS):
        group_bias = lax.dynamic_index_in_dim(bias, lay.plane ^ r, 1, keepdims=False)
        mixed_r, saved_r = attention_forward(hidden, attn_groups[r][:3], group_bias, counts)
        mixed.append(mixed_r)
        saved.append(saved_r)
    order = [lay.plane ^ place for place in range(GROUPS)]
    mixed = jnp.stack(mixed)
    mixed_true = jnp.concatenate([pick(mixed, r) for r in order], axis=1)
    out_groups = jnp.stack([group[3] for group in attn_groups])
    out_weight = jnp.concatenate([pick(out_groups, r) for r in order])
    middle = flat + nt(mixed_true, out_weight) + vectors[5]
    scaled_two, scale_two = normalize(middle)
    normed = (scaled_two * vectors[6] + vectors[7]).astype(BF16)

    normed_both = jnp.concatenate([normed, lay.swap(normed, 1)])
    place = lay.hidden_index()
    bias_up = vectors[9:].reshape(total, lay.block)[place].reshape(FF // 2)
    pre = nt(normed_both, up_full) + bias_up
    cdf = 0.5 * (1.0 + lax.erf(pre * (0.5**0.5)))
    active = (pre * cdf).astype(BF16)
    slope = cdf + pre * jnp.exp(-0.5 * pre * pre) * (1.0 / (2.0 * jnp.pi) ** 0.5)
    grad_down = lay.scatter_hidden(tn(active, back_both))
    part = nn(active, down_full)
    grad_pre = (nt(back_both, down_full) * slope).astype(BF16)
    grad_up = lay.scatter_hidden(tn(grad_pre, normed_both))
    grad_bias_up = jnp.sum(grad_pre.astype(F32), axis=0)
    back_part = nn(grad_pre, up_full)

    def both(value):
        return value[:rows] + lay.swap(value[rows:].astype(BF16), 1).astype(F32)

    result = (middle + both(part) + vectors[8]).astype(BF16)
    grad_normed = both(back_part)
    grad_middle = back.astype(F32) + norm_back(grad_normed, scaled_two, scale_two, vectors[6])
    branch = grad_middle.astype(BF16)
    grad_out = tn(branch, mixed_true).reshape(GROUPS, GROUP, D)
    grad_mixed = nn(branch, out_weight).astype(BF16).reshape(rows, GROUPS, GROUP)

    grads, grad_bias, grad_hidden = [], [], 0.0
    for r in range(GROUPS):
        grad_r = lax.dynamic_index_in_dim(grad_mixed, lay.plane ^ r, 1, keepdims=False)
        grad_parts = attention_backward(saved[r], grad_r)
        for part_index in range(3):
            grad_hidden = grad_hidden + nn(grad_parts[part_index], attn_groups[r][part_index])
        grads.append(
            jnp.stack([tn(value, hidden) for value in grad_parts] + [pick(grad_out, lay.plane ^ r)])
        )
        grad_bias.append(jnp.stack([jnp.sum(value.astype(F32), axis=0) for value in grad_parts]))
    grad_attn = lay.scatter_attention(grads)
    grad_bias = jnp.stack(grad_bias)
    grad_bias = jnp.concatenate([pick(grad_bias, r) for r in order], axis=1)
    input_grad = (grad_middle + norm_back(grad_hidden, scaled_one, scale_one, vectors[0])).astype(BF16)

    bias_up_rows = jnp.zeros((total, lay.block), F32).at[place].set(grad_bias_up.reshape(-1, lay.block))
    grad_vec = jnp.concatenate(
        [
            jnp.stack([jnp.sum(grad_hidden * scaled_one, axis=0), jnp.sum(grad_hidden, axis=0)]),
            grad_bias,
            jnp.stack(
                [
                    jnp.sum(grad_middle, axis=0),
                    jnp.sum(grad_normed * scaled_two, axis=0),
                    jnp.sum(grad_normed, axis=0),
                    jnp.sum(back.astype(F32), axis=0),
                ]
            ),
            bias_up_rows.reshape(4, D),
        ]
    )
    grad_vec = lax.psum(grad_vec, AXES)
    grad_attn, grad_up, grad_down = grad_attn.T, grad_up.T, grad_down.T
    attn_second_new, attn_new = adamw(attn_weight, attn_first, attn_second, grad_attn, 0.1)
    up_second_new, up_new = adamw(up_weight, up_first, up_second, grad_up, 0.1)
    down_second_new, down_new = adamw(down_weight, down_first, down_second, grad_down, 0.1)
    vec_second_new, vectors_new = adamw(vectors, vec_first, vec_second, grad_vec, 0.5)
    return (
        result.reshape(tokens.shape),
        input_grad.reshape(tokens.shape),
        grad_attn,
        grad_up,
        grad_down,
        grad_vec,
        attn_second_new,
        up_second_new,
        down_second_new,
        vec_second_new,
        attn_new,
        up_new,
        down_new,
        vectors_new,
    )


def solution(mesh):
    total = mesh.shape["wide"] * mesh.shape["narrow"]
    windows = P(None, AXES, None, None)
    counts = P(None, AXES)
    columns = P(None, AXES)
    in_specs = (windows,) * 2 + (counts,) * 2 + (columns,) * 9 + (P(),) * 3
    out_specs = (windows,) * 2 + (columns,) * 3 + (P(),) + (columns,) * 3 + (P(),) + (columns,) * 3 + (P(),)
    return jax.shard_map(
        functools.partial(per_device, total),
        mesh=mesh,
        in_specs=in_specs,
        out_specs=out_specs,
        check_vma=False,
    )
```

time: 690 us -> 475 us (0.69)
  waiting for transfers between devices: 473 us -> 89.6 us
  local copies, waits for them, and re-layouts: 36.7 us -> 116 us
  starting transfers between devices: 0.42 us -> 54.9 us
  matrix products: 81.1 us -> 105 us
  other arithmetic: 32.6 us -> 50.8 us
  between operations: 15.7 us -> 3.57 us
  blocking collectives: 40.3 us -> 49.4 us
    unnamed x9 -> x0, waiting for transfers between devices: 327 us -> none
    all_gather x3 -> x0, waiting for transfers between devices: 146 us -> none  [the longest x1 57 us: per_device(): lax.all_gather(shards[2], ('wide', 'narrow'), axis=1, tiled=True)]
    ppermute x0 -> x48, waiting for transfers between devices: none -> 89.6 us  [the longest x30 69.6 us: swap(): return lax.ppermute(value, AXES, [(i, i ^ mask) for i in range(self.total)])]
    ppermute x0 -> x48, starting transfers between devices: none -> 54.9 us  [the longest x18 32 us: shift(): return lax.ppermute(value, AXES, pairs)]
    reshape x12 -> x28, local copies, waits for them, and re-layouts: 0.08 us -> 41.1 us  [the longest x16 25 us: split_heads(): return rows.reshape(-1, SEQ, GROUP_HEADS, HEAD_DIM)]
    sub x0 -> x4, matrix products: none -> 16.9 us  [attention_forward(): exponent = jnp.exp(scores - top)]
    convert_element_type x2 -> x21, local copies, waits for them, and re-layouts: 3.73 us -> 14.6 us  [the longest x8 10.1 us: attention_forward(): return (mixed.reshape(hidden.shape[0], GROUP).astype(BF16), (q, k, v, prob))]
    psum x1, blocking collectives: 40.3 us -> 49.4 us  [per_device(): grad_vec = lax.psum(grad_vec, AXES)]
  transfers between devices with their start and end apart: 6 -> 48, of which waited for: 6 -> 16; matrix products, arithmetic and copies ran while one was open for 14% -> 39% of each run, Pallas kernels for 0% -> 0%
where the time goes in v1:
time: 475 us; the launch traced here: 469 us
  local copies, waits for them, and re-layouts  116 us (24%)
  matrix products  105 us (22%)
  waiting for transfers between devices  89.6 us (19%)
  starting transfers between devices  54.9 us (12%)
  other arithmetic  50.8 us (11%)
  blocking collectives  49.4 us (10%)
    ppermute x30, waiting for transfers between devices, swap(): return lax.ppermute(value, AXES, [(i, i ^ mask) for i in range(self.total)])  69.6 us
    psum x1, blocking collectives, per_device(): grad_vec = lax.psum(grad_vec, AXES)  49.4 us
    ppermute x18, starting transfers between devices, shift(): return lax.ppermute(value, AXES, pairs)  32 us
    dot_general x15, matrix products, nt(): lax.dot_general(left, right, (((1,), (1,)), ((), ())), preferred_element_...  30.5 us
    unnamed x332, local copies, waits for them, and re-layouts  25.9 us
    reshape x16, local copies, waits for them, and re-layouts, split_heads(): return rows.reshape(-1, SEQ, GROUP_HEADS, HEAD_DIM)  25 us
    ppermute x30, starting transfers between devices, swap(): return lax.ppermute(value, AXES, [(i, i ^ mask) for i in range(self.total)])  23 us
    ppermute x18, waiting for transfers between devices, shift(): return lax.ppermute(value, AXES, pairs)  20.1 us
  transfers between devices with their start and end apart: 48, of which 16 were waited for; matrix products, arithmetic and copies ran while one was open for 39% of the time, Pallas kernels for 0%

profile of v1, /device:TPU:0, one launch (start us, length us, event | category | flops | bytes accessed | tf_op | source)
XLA Modules:
  0.0 469.0 jit_solution(2492204919714821639)
XLA Ops:
  1.7 3.1 collective-permute-start.2
  4.8 2.6 collective-permute-start.1
  18.3 2.5 collective-permute-start.8
  23.2 8.5 %collective-permute-done.8 = bf16[4,80,640]{2,1,0:T(8,128)(2,1)} collective-permute-done((bf16[4,80,640]{2,1,0:T(8,128)(2,1)S(1)}, bf16[4,80,640]{2,1,0:T(8,128)(2,1)}, u32[]{:S(2)}, u32[]{:S(2)}) %collective-permute-start.8) | collective-permute-done | bytes 409632 | tf_op jit(solution)/shard_map/ppermute | solution.py:123
  32.9 7.1 %collective-permute-done.4 = bf16[4,80,640]{2,1,0:T(8,128)(2,1)} collective-permute-done((bf16[4,80,640]{2,1,0:T(8,128)(2,1)S(1)}, bf16[4,80,640]{2,1,0:T(8,128)(2,1)}, u32[]{:S(2)}, u32[]{:S(2)}) %collective-permute-start.4) | collective-permute-done | bytes 409632 | tf_op jit(solution)/shard_map/ppermute | solution.py:123
  43.0 5.7 %collective-permute-start.11 = (bf16[80,640]{1,0:T(8,128)(2,1)}, bf16[80,640]{1,0:T(8,128)(2,1)}, u32[]{:S(2)}, u32[]{:S(2)}) collective-permute-start(bf16[80,640]{1,0:T(8,128)(2,1)} %get-tuple-element.196), channel_id=1, source_target_pairs={{0,24},{1,25},{2,26},{3,27},{4,28},{5,29},{6,30},{7,31},{8,0},{9,1... | collective-permute-start | bytes 307208 | tf_op jit(solution)/shard_map/ppermute | solution.py:127
  54.8 1.9 reshape.1317
  59.2 2.0 convolution_add_fusion.12
  61.2 1.9 reshape.1319
  63.1 1.8 fusion.297
  66.7 1.9 reshape.1307
  72.8 1.9 reshape.1309
  74.7 1.8 fusion.301
  77.2 1.8 convolution_add_fusion.16
  78.9 1.9 reshape.1312
  85.1 1.9 reshape.1314
  99.2 4.1 fusion.304
  103.3 2.0 fusion.47
  116.1 4.1 fusion.309
  120.2 2.0 fusion.48
  131.3 4.6 fusion.314
  135.9 2.0 fusion.49
  140.4 1.9 fusion.34
  147.2 4.1 fusion.319
  151.4 2.0 fusion.50
  164.9 2.0 fusion.263
  166.9 2.5 collective-permute-start.16
  174.2 2.0 gather_fusion
  177.6 2.8 collective-permute-done.16
  180.4 8.1 %collective-permute-done.15 = bf16[4,80,640]{2,1,0:T(8,128)(2,1)} collective-permute-done((bf16[4,80,640]{2,1,0:T(8,128)(2,1)}, bf16[4,80,640]{2,1,0:T(8,128)(2,1)}, u32[]{:S(2)}, u32[]{:S(2)}) %collective-permute-start.15) | collective-permute-done | bytes 409632 | tf_op jit(solution)/shard_map/ppermute | solution.py:123
  190.2 5.9 %multiply_convert_fusion = (bf16[1024,1280]{1,0:T(8,128)(2,1)S(1)}, f32[1024,1280]{1,0:T(8,128)}) fusion(f32[1280]{0:T(1024)S(1)} %copy-done.136, bf16[1280,640]{1,0:T(8,128)(2,1)S(1)} %bitcast.614, bf16[512,640]{1,0:T(8,128)(2,1)} %collective-permute-done.10, bf16[512,640]{1,0:T(8,128)(2,1)} %add_convert_fusion.1), kind=kOutput, calls=%fused_computation.14 | convolution fusion | flops 1688207360 | bytes 10818560 | tf_op jit(solution)/shard_map/dot_general | solution.py:23
  196.1 4.5 convolution_convert_fusion
  200.8 2.4 collective-permute-start.44
  204.4 9.8 %collective-permute-done.44 = bf16[4,80,640]{2,1,0:T(8,128)(2,1)S(1)} collective-permute-done((bf16[4,80,640]{2,1,0:T(8,128)(2,1)S(1)}, bf16[4,80,640]{2,1,0:T(8,128)(2,1)S(1)}, u32[]{:S(2)}, u32[]{:S(2)}) %collective-permute-start.44) | collective-permute-done | bytes 409632 | tf_op jit(solution)/shard_map/ppermute | solution.py:123
  214.2 7.8 %collective-permute-done.43 = bf16[4,80,640]{2,1,0:T(8,128)(2,1)S(1)} collective-permute-done((bf16[4,80,640]{2,1,0:T(8,128)(2,1)S(1)}, bf16[4,80,640]{2,1,0:T(8,128)(2,1)S(1)}, u32[]{:S(2)}, u32[]{:S(2)}) %collective-permute-start.43) | collective-permute-done | bytes 409632 | tf_op jit(solution)/shard_map/ppermute | solution.py:123
  227.6 5.9 %collective-permute-done.46 = bf16[80,640]{1,0:T(8,128)(2,1)S(1)} collective-permute-done((bf16[80,640]{1,0:T(8,128)(2,1)S(1)}, bf16[80,640]{1,0:T(8,128)(2,1)S(1)}, u32[]{:S(2)}, u32[]{:S(2)}) %collective-permute-start.46) | collective-permute-done | bytes 102432 | tf_op jit(solution)/shard_map/ppermute | solution.py:127
  235.9 3.1 collective-permute-start.17
  239.0 2.9 collective-permute-done.19
  241.9 2.8 collective-permute-done.18
  245.7 2.5 collective-permute-start.22
  253.5 5.8 %collective-permute-done.22 = bf16[4,80,640]{2,1,0:T(8,128)(2,1)} collective-permute-done((bf16[4,80,640]{2,1,0:T(8,128)(2,1)}, bf16[4,80,640]{2,1,0:T(8,128)(2,1)}, u32[]{:S(2)}, u32[]{:S(2)}) %collective-permute-start.22) | collective-permute-done | bytes 409632 | tf_op jit(solution)/shard_map/ppermute | solution.py:123
  259.3 5.2 %collective-permute-done.21 = bf16[4,80,640]{2,1,0:T(8,128)(2,1)} collective-permute-done((bf16[4,80,640]{2,1,0:T(8,128)(2,1)}, bf16[4,80,640]{2,1,0:T(8,128)(2,1)}, u32[]{:S(2)}, u32[]{:S(2)}) %collective-permute-start.21) | collective-permute-done | bytes 409632 | tf_op jit(solution)/shard_map/ppermute | solution.py:123
  266.2 6.4 %convert_reduce_fusion = (f32[1280]{0:T(1024)}, bf16[1024,1280]{1,0:T(8,128)(2,1)S(1)}) fusion(f32[1024,1280]{1,0:T(8,128)} %get-tuple-element.253, f32[1280]{0:T(1024)S(1)} %copy-done.137, bf16[1280,640]{1,0:T(8,128)(2,1)S(1)} %bitcast.616, bf16[512,640]{1,0:T(8,128)(2,1)} %collective-permute-done.24, bf16[512,640]{1,0:T(8,128)(2,1)} %bitcast.67), kind=kOutput, calls=%fused_computation.13 | convolution fusion | flops 1697381120 | bytes 10823680 | tf_op jit(solution)/shard_map/dot_general | solution.py:23
  272.6 3.6 convolution_convert_fusion.1
  276.4 2.4 collective-permute-start.38
  279.9 2.2 fusion.326
  283.2 6.6 %collective-permute-done.38 = bf16[4,80,640]{2,1,0:T(8,128)(2,1)S(1)} collective-permute-done((bf16[4,80,640]{2,1,0:T(8,128)(2,1)S(1)}, bf16[4,80,640]{2,1,0:T(8,128)(2,1)S(1)}, u32[]{:S(2)}, u32[]{:S(2)}) %collective-permute-start.38) | collective-permute-done | bytes 409632 | tf_op jit(solution)/shard_map/ppermute | solution.py:123
  289.8 7.8 %collective-permute-done.37 = bf16[4,80,640]{2,1,0:T(8,128)(2,1)S(1)} collective-permute-done((bf16[4,80,640]{2,1,0:T(8,128)(2,1)S(1)}, bf16[4,80,640]{2,1,0:T(8,128)(2,1)S(1)}, u32[]{:S(2)}, u32[]{:S(2)}) %collective-permute-start.37) | collective-permute-done | bytes 409632 | tf_op jit(solution)/shard_map/ppermute | solution.py:123
  299.3 5.3 %collective-permute-start.41 = (bf16[80,640]{1,0:T(8,128)(2,1)}, bf16[80,640]{1,0:T(8,128)(2,1)}, u32[]{:S(2)}, u32[]{:S(2)}) collective-permute-start(bf16[80,640]{1,0:T(8,128)(2,1)} %get-tuple-element.128), channel_id=1, source_target_pairs={{0,24},{1,25},{2,26},{3,27},{4,28},{5,29},{6,30},{7,31},{8,0},{9,1... | collective-permute-start | bytes 307208 | tf_op jit(solution)/shard_map/ppermute | solution.py:127
  305.2 2.2 fusion.325
  314.2 2.3 multiply_subtract_fusion.1
  316.6 3.0 multiply_reduce_fusion.4
  319.6 4.1 fusion.272
  326.4 2.2 copy.140
  328.6 2.0 constant_dynamic-slice_fusion.23
  332.2 2.6 multiply_reduce_fusion.3
  339.9 2.6 multiply_reduce_fusion.2
  351.2 2.6 multiply_reduce_fusion
  359.0 2.6 multiply_reduce_fusion.1
  380.6 1.8 multiply_reduce_fusion.5
  392.5 2.7 add_convert_fusion
  396.6 2.6 collective-permute-start.32
  403.1 49.4 %psum.7 = f32[13,640]{1,0:T(8,128)S(1)} all-reduce(f32[13,640]{1,0:T(8,128)S(1)} %concatenate.138), channel_id=1, replica_groups=mesh['wide'=8,'narrow'=4] {'wide','narrow'}, use_global_device_ids=true, to_apply=%region_40.41 | all-reduce | flops 8320 | bytes 66560 | tf_op jit(solution)/shard_map/psum | solution.py:323
  461.2 6.4 %collective-permute-done.34 = bf16[80,640]{1,0:T(8,128)(2,1)S(1)} collective-permute-done((bf16[80,640]{1,0:T(8,128)(2,1)S(1)}, bf16[80,640]{1,0:T(8,128)(2,1)S(1)}, u32[]{:S(2)}, u32[]{:S(2)}) %collective-permute-start.34) | collective-permute-done | bytes 102432 | tf_op jit(solution)/shard_map/ppermute | solution.py:127
  (629 shorter events, 191.0 us)
Async XLA Ops:
  0.6 12.6 %copy-start.4 = (bf16[2,1,256,640]{3,2,1,0:T(8,128)(2,1)S(1)}, bf16[2,1,256,640]{3,2,1,0:T(8,128)(2,1)}, u32[]{:S(2)}) copy-start(bf16[2,1,256,640]{3,2,1,0:T(8,128)(2,1)} %param.16) | copy-start | bytes 1966084
  0.7 13.5 %copy-start.101 = (f32[13,640]{1,0:T(8,128)S(1)}, f32[13,640]{1,0:T(8,128)}, u32[]{:S(2)}) copy-start(f32[13,640]{1,0:T(8,128)} %param.29) | copy-start | bytes 99844
  0.7 13.6 %copy-start.145 = (s32[2,1]{0,1:T(1,128)S(1)}, s32[2,1]{0,1:T(1,128)}, u32[]{:S(2)}) copy-start(s32[2,1]{0,1:T(1,128)} %param.18) | copy-start | bytes 28
  0.7 13.6 %copy-start.146 = (s32[2,1]{0,1:T(1,128)S(1)}, s32[2,1]{0,1:T(1,128)}, u32[]{:S(2)}) copy-start(s32[2,1]{0,1:T(1,128)} %param.19) | copy-start | bytes 28
  1.7 14.0 %collective-permute-start.2 = (bf16[80,640]{1,0:T(8,128)(2,1)S(1)}, bf16[80,640]{1,0:T(8,128)(2,1)S(1)}, u32[]{:S(2)}, u32[]{:S(2)}) collective-permute-start(bf16[80,640]{1,0:T(8,128)(2,1)S(1)} %get-tuple-element.198), channel_id=1, source_target_pairs={{0,8},{1,9},{2,10},{3,11},{4,12},{5,13},{6,14},{7,15},{8,16},{9,17... | collective-permute-start | bytes 307208 | tf_op jit(solution)/shard_map/ppermute | solution.py:127
  4.8 10.9 %collective-permute-start.1 = (bf16[80,640]{1,0:T(8,128)(2,1)S(1)}, bf16[80,640]{1,0:T(8,128)(2,1)S(1)}, u32[]{:S(2)}, u32[]{:S(2)}) collective-permute-start(bf16[80,640]{1,0:T(8,128)(2,1)S(1)} %get-tuple-element.198), channel_id=1, source_target_pairs={{0,16},{1,17},{2,18},{3,19},{4,20},{5,21},{6,22},{7,23},{8,24},{9,... | collective-permute-start | bytes 307208 | tf_op jit(solution)/shard_map/ppermute | solution.py:127
  7.4 8.4 %collective-permute-start = (bf16[80,640]{1,0:T(8,128)(2,1)S(1)}, bf16[80,640]{1,0:T(8,128)(2,1)S(1)}, u32[]{:S(2)}, u32[]{:S(2)}) collective-permute-start(bf16[80,640]{1,0:T(8,128)(2,1)S(1)} %get-tuple-element.198), channel_id=1, source_target_pairs={{0,24},{1,25},{2,26},{3,27},{4,28},{5,29},{6,30},{7,31},{8,0},{9,1... | collective-permute-start | bytes 307208 | tf_op jit(solution)/shard_map/ppermute | solution.py:127
  10.3 154.6 %collective-permute-start.13 = (bf16[80,640]{1,0:T(8,128)(2,1)}, bf16[80,640]{1,0:T(8,128)(2,1)}, u32[]{:S(2)}, u32[]{:S(2)}) collective-permute-start(bf16[80,640]{1,0:T(8,128)(2,1)} %get-tuple-element.196), channel_id=1, source_target_pairs={{0,8},{1,9},{2,10},{3,11},{4,12},{5,13},{6,14},{7,15},{8,16},{9,17... | collective-permute-start | bytes 307208 | tf_op jit(solution)/shard_map/ppermute | solution.py:127
  11.0 153.9 %collective-permute-start.12 = (bf16[80,640]{1,0:T(8,128)(2,1)}, bf16[80,640]{1,0:T(8,128)(2,1)}, u32[]{:S(2)}, u32[]{:S(2)}) collective-permute-start(bf16[80,640]{1,0:T(8,128)(2,1)} %get-tuple-element.196), channel_id=1, source_target_pairs={{0,16},{1,17},{2,18},{3,19},{4,20},{5,21},{6,22},{7,23},{8,24},{9,... | collective-permute-start | bytes 307208 | tf_op jit(solution)/shard_map/ppermute | solution.py:127
  15.8 5.6 %collective-permute-start.3 = (bf16[4,80,640]{2,1,0:T(8,128)(2,1)S(1)}, bf16[4,80,640]{2,1,0:T(8,128)(2,1)S(1)}, u32[]{:S(2)}, u32[]{:S(2)}) collective-permute-start(bf16[4,80,640]{2,1,0:T(8,128)(2,1)S(1)} %pad_maximum_fusion.15), channel_id=1, source_target_pairs={{0,1},{1,0},{2,3},{3,2},{4,5},{5,4},{6,7},{7,6},{8,9},{9,8},{10,11... | collective-permute-start | bytes 1228808 | tf_op jit(solution)/shard_map/ppermute | solution.py:123
  18.3 13.4 %collective-permute-start.8 = (bf16[4,80,640]{2,1,0:T(8,128)(2,1)S(1)}, bf16[4,80,640]{2,1,0:T(8,128)(2,1)}, u32[]{:S(2)}, u32[]{:S(2)}) collective-permute-start(bf16[4,80,640]{2,1,0:T(8,128)(2,1)S(1)} %pad_maximum_fusion.15), channel_id=1, source_target_pairs={{0,6},{1,7},{2,4},{3,5},{4,2},{5,3},{6,0},{7,1},{8,14},{9,15},{10,... | collective-permute-start | bytes 1228808 | tf_op jit(solution)/shard_map/ppermute | solution.py:123
  20.8 22.2 %collective-permute-start.6 = (bf16[4,80,640]{2,1,0:T(8,128)(2,1)S(1)}, bf16[4,80,640]{2,1,0:T(8,128)(2,1)}, u32[]{:S(2)}, u32[]{:S(2)}) collective-permute-start(bf16[4,80,640]{2,1,0:T(8,128)(2,1)S(1)} %pad_maximum_fusion.15), channel_id=1, source_target_pairs={{0,4},{1,5},{2,6},{3,7},{4,0},{5,1},{6,2},{7,3},{8,12},{9,13},{10,... | collective-permute-start | bytes 1228808 | tf_op jit(solution)/shard_map/ppermute | solution.py:123
  21.4 18.6 %collective-permute-start.4 = (bf16[4,80,640]{2,1,0:T(8,128)(2,1)S(1)}, bf16[4,80,640]{2,1,0:T(8,128)(2,1)}, u32[]{:S(2)}, u32[]{:S(2)}) collective-permute-start(bf16[4,80,640]{2,1,0:T(8,128)(2,1)S(1)} %pad_maximum_fusion.15), channel_id=1, source_target_pairs={{0,2},{1,3},{2,0},{3,1},{4,6},{5,7},{6,4},{7,5},{8,10},{9,11},{10,... | collective-permute-start | bytes 1228808 | tf_op jit(solution)/shard_map/ppermute | solution.py:123
  22.4 9.4 %copy-start.18 = (f32[512,160]{0,1:T(8,128)}, f32[512,160]{0,1:T(8,128)S(1)}, u32[]{:S(2)}) copy-start(f32[512,160]{0,1:T(8,128)S(1)} %convolution_add_fusion.21) | copy-start | bytes 983044
  23.0 17.2 %copy-start.20 = (f32[512,160]{0,1:T(8,128)}, f32[512,160]{0,1:T(8,128)S(1)}, u32[]{:S(2)}) copy-start(f32[512,160]{0,1:T(8,128)S(1)} %convolution_add_fusion.22) | copy-start | bytes 983044
  31.7 18.5 %collective-permute-start.9 = (bf16[4,80,640]{2,1,0:T(8,128)(2,1)}, bf16[4,80,640]{2,1,0:T(8,128)(2,1)}, u32[]{:S(2)}, u32[]{:S(2)}) collective-permute-start(bf16[4,80,640]{2,1,0:T(8,128)(2,1)} %collective-permute-done.8), channel_id=1, source_target_pairs={{0,1},{1,0},{2,3},{3,2},{4,5},{5,4},{6,7},{7,6},{8,9},{9,8},{10,11... | collective-permute-start | bytes 1228808 | tf_op jit(solution)/shard_map/ppermute | solution.py:123
  40.0 8.7 %collective-permute-start.5 = (bf16[4,80,640]{2,1,0:T(8,128)(2,1)}, bf16[4,80,640]{2,1,0:T(8,128)(2,1)}, u32[]{:S(2)}, u32[]{:S(2)}) collective-permute-start(bf16[4,80,640]{2,1,0:T(8,128)(2,1)} %collective-permute-done.4), channel_id=1, source_target_pairs={{0,1},{1,0},{2,3},{3,2},{4,5},{5,4},{6,7},{7,6},{8,9},{9,8},{10,11... | collective-permute-start | bytes 1228808 | tf_op jit(solution)/shard_map/ppermute | solution.py:123
  43.0 121.9 %collective-permute-start.11 = (bf16[80,640]{1,0:T(8,128)(2,1)}, bf16[80,640]{1,0:T(8,128)(2,1)}, u32[]{:S(2)}, u32[]{:S(2)}) collective-permute-start(bf16[80,640]{1,0:T(8,128)(2,1)} %get-tuple-element.196), channel_id=1, source_target_pairs={{0,24},{1,25},{2,26},{3,27},{4,28},{5,29},{6,30},{7,31},{8,0},{9,1... | collective-permute-start | bytes 307208 | tf_op jit(solution)/shard_map/ppermute | solution.py:127
  48.7 2.7 collective-permute-start.7
  155.9 6.2 %copy-start.79 = (bf16[160,640]{1,0:T(8,128)(2,1)S(1)}, bf16[160,640]{1,0:T(8,128)(2,1)}, u32[]{:S(2)}) copy-start(bf16[160,640]{1,0:T(8,128)(2,1)} %get-tuple-element.107) | copy-start | bytes 614404
  164.6 25.6 %collective-permute-start.10 = (bf16[512,640]{1,0:T(8,128)(2,1)}, bf16[512,640]{1,0:T(8,128)(2,1)}, u32[]{:S(2)}, u32[]{:S(2)}) collective-permute-start(bf16[512,640]{1,0:T(8,128)(2,1)} %add_convert_fusion.1), channel_id=1, source_target_pairs={{0,1},{1,0},{2,3},{3,2},{4,5},{5,4},{6,7},{7,6},{8,9},{9,8},{10,11... | collective-permute-start | bytes 1966088 | tf_op jit(solution)/shard_map/ppermute | solution.py:123
  166.9 13.6 %collective-permute-start.16 = (bf16[4,80,640]{2,1,0:T(8,128)(2,1)}, bf16[4,80,640]{2,1,0:T(8,128)(2,1)}, u32[]{:S(2)}, u32[]{:S(2)}) collective-permute-start(bf16[4,80,640]{2,1,0:T(8,128)(2,1)} %get-tuple-element.152), channel_id=1, source_target_pairs={{0,6},{1,7},{2,4},{3,5},{4,2},{5,3},{6,0},{7,1},{8,14},{9,15},{10,... | collective-permute-start | bytes 1228808 | tf_op jit(solution)/shard_map/ppermute | solution.py:123
  169.3 19.2 %collective-permute-start.15 = (bf16[4,80,640]{2,1,0:T(8,128)(2,1)}, bf16[4,80,640]{2,1,0:T(8,128)(2,1)}, u32[]{:S(2)}, u32[]{:S(2)}) collective-permute-start(bf16[4,80,640]{2,1,0:T(8,128)(2,1)} %get-tuple-element.152), channel_id=1, source_target_pairs={{0,4},{1,5},{2,6},{3,7},{4,0},{5,1},{6,2},{7,3},{8,12},{9,13},{10,... | collective-permute-start | bytes 1228808 | tf_op jit(solution)/shard_map/ppermute | solution.py:123
  169.9 18.7 %collective-permute-start.14 = (bf16[4,80,640]{2,1,0:T(8,128)(2,1)}, bf16[4,80,640]{2,1,0:T(8,128)(2,1)}, u32[]{:S(2)}, u32[]{:S(2)}) collective-permute-start(bf16[4,80,640]{2,1,0:T(8,128)(2,1)} %get-tuple-element.152), channel_id=1, source_target_pairs={{0,2},{1,3},{2,0},{3,1},{4,6},{5,7},{6,4},{7,5},{8,10},{9,11},{10,... | collective-permute-start | bytes 1228808 | tf_op jit(solution)/shard_map/ppermute | solution.py:123
  170.4 25.7 %collective-permute-start.24 = (bf16[512,640]{1,0:T(8,128)(2,1)}, bf16[512,640]{1,0:T(8,128)(2,1)}, u32[]{:S(2)}, u32[]{:S(2)}) collective-permute-start(bf16[512,640]{1,0:T(8,128)(2,1)} %bitcast.67), channel_id=1, source_target_pairs={{0,1},{1,0},{2,3},{3,2},{4,5},{5,4},{6,7},{7,6},{8,9},{9,8},{10,11... | collective-permute-start | bytes 1966088 | tf_op jit(solution)/shard_map/ppermute | solution.py:123
  200.8 13.4 %collective-permute-start.44 = (bf16[4,80,640]{2,1,0:T(8,128)(2,1)S(1)}, bf16[4,80,640]{2,1,0:T(8,128)(2,1)S(1)}, u32[]{:S(2)}, u32[]{:S(2)}) collective-permute-start(bf16[4,80,640]{2,1,0:T(8,128)(2,1)S(1)} %bitcast.686), channel_id=1, source_target_pairs={{0,6},{1,7},{2,4},{3,5},{4,2},{5,3},{6,0},{7,1},{8,14},{9,15},{10,... | collective-permute-start | bytes 1228808 | tf_op jit(solution)/shard_map/ppermute | solution.py:123
  203.2 18.7 %collective-permute-start.43 = (bf16[4,80,640]{2,1,0:T(8,128)(2,1)S(1)}, bf16[4,80,640]{2,1,0:T(8,128)(2,1)S(1)}, u32[]{:S(2)}, u32[]{:S(2)}) collective-permute-start(bf16[4,80,640]{2,1,0:T(8,128)(2,1)S(1)} %bitcast.685), channel_id=1, source_target_pairs={{0,4},{1,5},{2,6},{3,7},{4,0},{5,1},{6,2},{7,3},{8,12},{9,13},{10,... | collective-permute-start | bytes 1228808 | tf_op jit(solution)/shard_map/ppermute | solution.py:123
  203.8 18.2 %collective-permute-start.42 = (bf16[4,80,640]{2,1,0:T(8,128)(2,1)S(1)}, bf16[4,80,640]{2,1,0:T(8,128)(2,1)S(1)}, u32[]{:S(2)}, u32[]{:S(2)}) collective-permute-start(bf16[4,80,640]{2,1,0:T(8,128)(2,1)S(1)} %bitcast.684), channel_id=1, source_target_pairs={{0,2},{1,3},{2,0},{3,1},{4,6},{5,7},{6,4},{7,5},{8,10},{9,11},{10,... | collective-permute-start | bytes 1228808 | tf_op jit(solution)/shard_map/ppermute | solution.py:123
  221.9 11.5 %copy-start.83 = (f32[640,80]{0,1:T(8,128)S(1)}, f32[640,80]{0,1:T(8,128)}, u32[]{:S(2)}) copy-start(f32[640,80]{0,1:T(8,128)} %param.26) | copy-start | bytes 614404
  221.9 11.5 %copy-start.84 = (f32[640,80]{0,1:T(8,128)S(1)}, f32[640,80]{0,1:T(8,128)}, u32[]{:S(2)}) copy-start(f32[640,80]{0,1:T(8,128)} %param.27) | copy-start | bytes 614404
  221.9 11.5 %copy-start.85 = (f32[640,80]{0,1:T(8,128)S(1)}, f32[640,80]{0,1:T(8,128)}, u32[]{:S(2)}) copy-start(f32[640,80]{0,1:T(8,128)} %param.28) | copy-start | bytes 614404
  222.2 5.4 %collective-permute-start.47 = (bf16[80,640]{1,0:T(8,128)(2,1)S(1)}, bf16[80,640]{1,0:T(8,128)(2,1)S(1)}, u32[]{:S(2)}, u32[]{:S(2)}) collective-permute-start(bf16[80,640]{1,0:T(8,128)(2,1)S(1)} %get-tuple-element.125), channel_id=1, source_target_pairs={{0,24},{1,25},{2,26},{3,27},{4,28},{5,29},{6,30},{7,31},{8,0},{9,1... | collective-permute-start | bytes 307208 | tf_op jit(solution)/shard_map/ppermute | solution.py:127
  222.8 10.6 %collective-permute-start.46 = (bf16[80,640]{1,0:T(8,128)(2,1)S(1)}, bf16[80,640]{1,0:T(8,128)(2,1)S(1)}, u32[]{:S(2)}, u32[]{:S(2)}) collective-permute-start(bf16[80,640]{1,0:T(8,128)(2,1)S(1)} %get-tuple-element.126), channel_id=1, source_target_pairs={{0,16},{1,17},{2,18},{3,19},{4,20},{5,21},{6,22},{7,23},{8,24},{9,... | collective-permute-start | bytes 307208 | tf_op jit(solution)/shard_map/ppermute | solution.py:127
  224.2 9.3 %collective-permute-start.45 = (bf16[80,640]{1,0:T(8,128)(2,1)S(1)}, bf16[80,640]{1,0:T(8,128)(2,1)S(1)}, u32[]{:S(2)}, u32[]{:S(2)}) collective-permute-start(bf16[80,640]{1,0:T(8,128)(2,1)S(1)} %get-tuple-element.124), channel_id=1, source_target_pairs={{0,8},{1,9},{2,10},{3,11},{4,12},{5,13},{6,14},{7,15},{8,16},{9,17... | collective-permute-start | bytes 307208 | tf_op jit(solution)/shard_map/ppermute | solution.py:127
  234.4 7.5 %collective-permute-start.19 = (bf16[80,640]{1,0:T(8,128)(2,1)S(1)}, bf16[80,640]{1,0:T(8,128)(2,1)S(1)}, u32[]{:S(2)}, u32[]{:S(2)}) collective-permute-start(bf16[80,640]{1,0:T(8,128)(2,1)S(1)} %get-tuple-element.194), channel_id=1, source_target_pairs={{0,8},{1,9},{2,10},{3,11},{4,12},{5,13},{6,14},{7,15},{8,16},{9,17... | collective-permute-start | bytes 307208 | tf_op jit(solution)/shard_map/ppermute | solution.py:127
  234.4 10.3 %collective-permute-start.18 = (bf16[80,640]{1,0:T(8,128)(2,1)S(1)}, bf16[80,640]{1,0:T(8,128)(2,1)S(1)}, u32[]{:S(2)}, u32[]{:S(2)}) collective-permute-start(bf16[80,640]{1,0:T(8,128)(2,1)S(1)} %get-tuple-element.194), channel_id=1, source_target_pairs={{0,16},{1,17},{2,18},{3,19},{4,20},{5,21},{6,22},{7,23},{8,24},{9,... | collective-permute-start | bytes 307208 | tf_op jit(solution)/shard_map/ppermute | solution.py:127
  235.9 8.8 %collective-permute-start.17 = (bf16[80,640]{1,0:T(8,128)(2,1)S(1)}, bf16[80,640]{1,0:T(8,128)(2,1)S(1)}, u32[]{:S(2)}, u32[]{:S(2)}) collective-permute-start(bf16[80,640]{1,0:T(8,128)(2,1)S(1)} %get-tuple-element.194), channel_id=1, source_target_pairs={{0,24},{1,25},{2,26},{3,27},{4,28},{5,29},{6,30},{7,31},{8,0},{9,1... | collective-permute-start | bytes 307208 | tf_op jit(solution)/shard_map/ppermute | solution.py:127
  245.7 13.6 %collective-permute-start.22 = (bf16[4,80,640]{2,1,0:T(8,128)(2,1)}, bf16[4,80,640]{2,1,0:T(8,128)(2,1)}, u32[]{:S(2)}, u32[]{:S(2)}) collective-permute-start(bf16[4,80,640]{2,1,0:T(8,128)(2,1)} %get-tuple-element.150), channel_id=1, source_target_pairs={{0,6},{1,7},{2,4},{3,5},{4,2},{5,3},{6,0},{7,1},{8,14},{9,15},{10,... | collective-permute-start | bytes 1228808 | tf_op jit(solution)/shard_map/ppermute | solution.py:123
  248.1 16.4 %collective-permute-start.21 = (bf16[4,80,640]{2,1,0:T(8,128)(2,1)}, bf16[4,80,640]{2,1,0:T(8,128)(2,1)}, u32[]{:S(2)}, u32[]{:S(2)}) collective-permute-start(bf16[4,80,640]{2,1,0:T(8,128)(2,1)} %get-tuple-element.150), channel_id=1, source_target_pairs={{0,4},{1,5},{2,6},{3,7},{4,0},{5,1},{6,2},{7,3},{8,12},{9,13},{10,... | collective-permute-start | bytes 1228808 | tf_op jit(solution)/shard_map/ppermute | solution.py:123
  248.7 15.9 %collective-permute-start.20 = (bf16[4,80,640]{2,1,0:T(8,128)(2,1)}, bf16[4,80,640]{2,1,0:T(8,128)(2,1)}, u32[]{:S(2)}, u32[]{:S(2)}) collective-permute-start(bf16[4,80,640]{2,1,0:T(8,128)(2,1)} %get-tuple-element.150), channel_id=1, source_target_pairs={{0,2},{1,3},{2,0},{3,1},{4,6},{5,7},{6,4},{7,5},{8,10},{9,11},{10,... | collective-permute-start | bytes 1228808 | tf_op jit(solution)/shard_map/ppermute | solution.py:123
  276.4 13.4 %collective-permute-start.38 = (bf16[4,80,640]{2,1,0:T(8,128)(2,1)S(1)}, bf16[4,80,640]{2,1,0:T(8,128)(2,1)S(1)}, u32[]{:S(2)}, u32[]{:S(2)}) collective-permute-start(bf16[4,80,640]{2,1,0:T(8,128)(2,1)S(1)} %bitcast.683), channel_id=1, source_target_pairs={{0,6},{1,7},{2,4},{3,5},{4,2},{5,3},{6,0},{7,1},{8,14},{9,15},{10,... | collective-permute-start | bytes 1228808 | tf_op jit(solution)/shard_map/ppermute | solution.py:123
  278.8 18.7 %collective-permute-start.37 = (bf16[4,80,640]{2,1,0:T(8,128)(2,1)S(1)}, bf16[4,80,640]{2,1,0:T(8,128)(2,1)S(1)}, u32[]{:S(2)}, u32[]{:S(2)}) collective-permute-start(bf16[4,80,640]{2,1,0:T(8,128)(2,1)S(1)} %bitcast.682), channel_id=1, source_target_pairs={{0,4},{1,5},{2,6},{3,7},{4,0},{5,1},{6,2},{7,3},{8,12},{9,13},{10,... | collective-permute-start | bytes 1228808 | tf_op jit(solution)/shard_map/ppermute | solution.py:123
  279.3 18.2 %collective-permute-start.36 = (bf16[4,80,640]{2,1,0:T(8,128)(2,1)S(1)}, bf16[4,80,640]{2,1,0:T(8,128)(2,1)S(1)}, u32[]{:S(2)}, u32[]{:S(2)}) collective-permute-start(bf16[4,80,640]{2,1,0:T(8,128)(2,1)S(1)} %bitcast.681), channel_id=1, source_target_pairs={{0,2},{1,3},{2,0},{3,1},{4,6},{5,7},{6,4},{7,5},{8,10},{9,11},{10,... | collective-permute-start | bytes 1228808 | tf_op jit(solution)/shard_map/ppermute | solution.py:123
  282.2 16.5 %copy-start.10 = (f32[1024,640]{1,0:T(8,128)}, f32[1024,640]{1,0:T(8,128)S(1)}, u32[]{:S(2)}) copy-start(f32[1024,640]{1,0:T(8,128)S(1)} %fusion.326) | copy-start | bytes 7864324
  283.2 33.4 %collective-permute-start.25 = (bf16[512,640]{1,0:T(8,128)(2,1)}, bf16[512,640]{1,0:T(8,128)(2,1)}, u32[]{:S(2)}, u32[]{:S(2)}) collective-permute-start(bf16[512,640]{1,0:T(8,128)(2,1)} %slice.456), channel_id=1, source_target_pairs={{0,1},{1,0},{2,3},{3,2},{4,5},{5,4},{6,7},{7,6},{8,9},{9,8},{10,11... | collective-permute-start | bytes 1966088 | tf_op jit(solution)/shard_map/ppermute | solution.py:123
  297.5 7.7 %copy-start.148 = (bf16[1024,1280]{1,0:T(8,128)(2,1)S(1)}, bf16[1024,1280]{1,0:T(8,128)(2,1)}, u32[]{:S(2)}) copy-start(bf16[1024,1280]{1,0:T(8,128)(2,1)} %copy-done.147) | copy-start | bytes 7864324
  299.3 14.8 %collective-permute-start.41 = (bf16[80,640]{1,0:T(8,128)(2,1)}, bf16[80,640]{1,0:T(8,128)(2,1)}, u32[]{:S(2)}, u32[]{:S(2)}) collective-permute-start(bf16[80,640]{1,0:T(8,128)(2,1)} %get-tuple-element.128), channel_id=1, source_target_pairs={{0,24},{1,25},{2,26},{3,27},{4,28},{5,29},{6,30},{7,31},{8,0},{9,1... | collective-permute-start | bytes 307208 | tf_op jit(solution)/shard_map/ppermute | solution.py:127
  304.6 9.6 %collective-permute-start.40 = (bf16[80,640]{1,0:T(8,128)(2,1)}, bf16[80,640]{1,0:T(8,128)(2,1)}, u32[]{:S(2)}, u32[]{:S(2)}) collective-permute-start(bf16[80,640]{1,0:T(8,128)(2,1)} %get-tuple-element.129), channel_id=1, source_target_pairs={{0,16},{1,17},{2,18},{3,19},{4,20},{5,21},{6,22},{7,23},{8,24},{9,... | collective-permute-start | bytes 307208 | tf_op jit(solution)/shard_map/ppermute | solution.py:127
  304.6 9.6 %collective-permute-start.39 = (bf16[80,640]{1,0:T(8,128)(2,1)}, bf16[80,640]{1,0:T(8,128)(2,1)}, u32[]{:S(2)}, u32[]{:S(2)}) collective-permute-start(bf16[80,640]{1,0:T(8,128)(2,1)} %get-tuple-element.127), channel_id=1, source_target_pairs={{0,8},{1,9},{2,10},{3,11},{4,12},{5,13},{6,14},{7,15},{8,16},{9,17... | collective-permute-start | bytes 307208 | tf_op jit(solution)/shard_map/ppermute | solution.py:127
  309.8 9.7 %collective-permute-start.23 = (bf16[512,640]{1,0:T(8,128)(2,1)}, bf16[512,640]{1,0:T(8,128)(2,1)}, u32[]{:S(2)}, u32[]{:S(2)}) collective-permute-start(bf16[512,640]{1,0:T(8,128)(2,1)} %slice.457), channel_id=1, source_target_pairs={{0,1},{1,0},{2,3},{3,2},{4,5},{5,4},{6,7},{7,6},{8,9},{9,8},{10,11... | collective-permute-start | bytes 1966088 | tf_op jit(solution)/shard_map/ppermute | solution.py:123
  384.4 10.8 %collective-permute-start.31 = (bf16[4,80,640]{2,1,0:T(8,128)(2,1)}, bf16[4,80,640]{2,1,0:T(8,128)(2,1)}, u32[]{:S(2)}, u32[]{:S(2)}) collective-permute-start(bf16[4,80,640]{2,1,0:T(8,128)(2,1)} %dynamic-slice_bitcast_fusion), channel_id=1, source_target_pairs={{0,1},{1,0},{2,3},{3,2},{4,5},{5,4},{6,7},{7,6},{8,9},{9,8},{10,11... | collective-permute-start | bytes 1228808 | tf_op jit(solution)/shard_map/ppermute | solution.py:123
  386.9 12.3 %collective-permute-start.29 = (bf16[4,80,640]{2,1,0:T(8,128)(2,1)}, bf16[4,80,640]{2,1,0:T(8,128)(2,1)}, u32[]{:S(2)}, u32[]{:S(2)}) collective-permute-start(bf16[4,80,640]{2,1,0:T(8,128)(2,1)} %dynamic-slice_bitcast_fusion.1), channel_id=1, source_target_pairs={{0,1},{1,0},{2,3},{3,2},{4,5},{5,4},{6,7},{7,6},{8,9},{9,8},{10,11... | collective-permute-start | bytes 1228808 | tf_op jit(solution)/shard_map/ppermute | solution.py:123
  388.9 12.2 %collective-permute-start.27 = (bf16[4,80,640]{2,1,0:T(8,128)(2,1)}, bf16[4,80,640]{2,1,0:T(8,128)(2,1)}, u32[]{:S(2)}, u32[]{:S(2)}) collective-permute-start(bf16[4,80,640]{2,1,0:T(8,128)(2,1)} %dynamic-slice_bitcast_fusion.2), channel_id=1, source_target_pairs={{0,1},{1,0},{2,3},{3,2},{4,5},{5,4},{6,7},{7,6},{8,9},{9,8},{10,11... | collective-permute-start | bytes 1228808 | tf_op jit(solution)/shard_map/ppermute | solution.py:123
  391.4 61.1 %collective-permute-start.26 = (bf16[4,80,640]{2,1,0:T(8,128)(2,1)}, bf16[4,80,640]{2,1,0:T(8,128)(2,1)}, u32[]{:S(2)}, u32[]{:S(2)}) collective-permute-start(bf16[4,80,640]{2,1,0:T(8,128)(2,1)} %dynamic-slice_bitcast_fusion.3), channel_id=1, source_target_pairs={{0,1},{1,0},{2,3},{3,2},{4,5},{5,4},{6,7},{7,6},{8,9},{9,8},{10,11... | collective-permute-start | bytes 1228808 | tf_op jit(solution)/shard_map/ppermute | solution.py:123
  396.6 57.1 %collective-permute-start.32 = (bf16[4,80,640]{2,1,0:T(8,128)(2,1)S(1)}, bf16[4,80,640]{2,1,0:T(8,128)(2,1)}, u32[]{:S(2)}, u32[]{:S(2)}) collective-permute-start(bf16[4,80,640]{2,1,0:T(8,128)(2,1)S(1)} %pad_maximum_fusion.20), channel_id=1, source_target_pairs={{0,6},{1,7},{2,4},{3,5},{4,2},{5,3},{6,0},{7,1},{8,14},{9,15},{10,... | collective-permute-start | bytes 1228808 | tf_op jit(solution)/shard_map/ppermute | solution.py:123
  400.5 53.2 %collective-permute-start.30 = (bf16[4,80,640]{2,1,0:T(8,128)(2,1)S(1)}, bf16[4,80,640]{2,1,0:T(8,128)(2,1)}, u32[]{:S(2)}, u32[]{:S(2)}) collective-permute-start(bf16[4,80,640]{2,1,0:T(8,128)(2,1)S(1)} %pad_maximum_fusion.19), channel_id=1, source_target_pairs={{0,4},{1,5},{2,6},{3,7},{4,0},{5,1},{6,2},{7,3},{8,12},{9,13},{10,... | collective-permute-start | bytes 1228808 | tf_op jit(solution)/shard_map/ppermute | solution.py:123
  402.3 51.4 %collective-permute-start.28 = (bf16[4,80,640]{2,1,0:T(8,128)(2,1)S(1)}, bf16[4,80,640]{2,1,0:T(8,128)(2,1)S(1)}, u32[]{:S(2)}, u32[]{:S(2)}) collective-permute-start(bf16[4,80,640]{2,1,0:T(8,128)(2,1)S(1)} %pad_maximum_fusion.18), channel_id=1, source_target_pairs={{0,2},{1,3},{2,0},{3,1},{4,6},{5,7},{6,4},{7,5},{8,10},{9,11},{10,... | collective-permute-start | bytes 1228808 | tf_op jit(solution)/shard_map/ppermute | solution.py:123
  452.5 7.7 %copy-start.100 = (f32[13,640]{1,0:T(8,128)}, f32[13,640]{1,0:T(8,128)S(1)}, u32[]{:S(2)}) copy-start(f32[13,640]{1,0:T(8,128)S(1)} %psum.7) | copy-start | bytes 99844
  454.5 13.2 %copy-start.50 = (f32[640,80]{0,1:T(8,128)S(1)}, f32[640,80]{0,1:T(8,128)}, u32[]{:S(2)}) copy-start(f32[640,80]{0,1:T(8,128)} %param.20) | copy-start | bytes 614404
  454.5 13.2 %copy-start.81 = (f32[640,80]{0,1:T(8,128)S(1)}, f32[640,80]{0,1:T(8,128)}, u32[]{:S(2)}) copy-start(f32[640,80]{0,1:T(8,128)} %param.21) | copy-start | bytes 614404
  454.5 13.1 %copy-start.82 = (f32[640,80]{0,1:T(8,128)S(1)}, f32[640,80]{0,1:T(8,128)}, u32[]{:S(2)}) copy-start(f32[640,80]{0,1:T(8,128)} %param.22) | copy-start | bytes 614404
  456.1 5.1 %collective-permute-start.35 = (bf16[80,640]{1,0:T(8,128)(2,1)S(1)}, bf16[80,640]{1,0:T(8,128)(2,1)S(1)}, u32[]{:S(2)}, u32[]{:S(2)}) collective-permute-start(bf16[80,640]{1,0:T(8,128)(2,1)S(1)} %get-tuple-element.131), channel_id=1, source_target_pairs={{0,24},{1,25},{2,26},{3,27},{4,28},{5,29},{6,30},{7,31},{8,0},{9,1... | collective-permute-start | bytes 307208 | tf_op jit(solution)/shard_map/ppermute | solution.py:127
  457.7 10.0 %collective-permute-start.34 = (bf16[80,640]{1,0:T(8,128)(2,1)S(1)}, bf16[80,640]{1,0:T(8,128)(2,1)S(1)}, u32[]{:S(2)}, u32[]{:S(2)}) collective-permute-start(bf16[80,640]{1,0:T(8,128)(2,1)S(1)} %get-tuple-element.132), channel_id=1, source_target_pairs={{0,16},{1,17},{2,18},{3,19},{4,20},{5,21},{6,22},{7,23},{8,24},{9,... | collective-permute-start | bytes 307208 | tf_op jit(solution)/shard_map/ppermute | solution.py:127
  458.9 8.8 %collective-permute-start.33 = (bf16[80,640]{1,0:T(8,128)(2,1)S(1)}, bf16[80,640]{1,0:T(8,128)(2,1)S(1)}, u32[]{:S(2)}, u32[]{:S(2)}) collective-permute-start(bf16[80,640]{1,0:T(8,128)(2,1)S(1)} %get-tuple-element.130), channel_id=1, source_target_pairs={{0,8},{1,9},{2,10},{3,11},{4,12},{5,13},{6,14},{7,15},{8,16},{9,17... | collective-permute-start | bytes 307208 | tf_op jit(solution)/shard_map/ppermute | solution.py:127
  (133 other events, 307.1 us)
